TPU v7x, 512 devices: a whole 4x8x8 slice. The times are simulated.
512 devices in a mesh: row: 32 (over y, x), col: 16 (over z, core).
Axes of the slice: x: 4, y: 8, z: 8, core: 2. Of those that a mesh axis runs over, the one named last changes fastest.
Arguments:
- choi: float32 [4, 8192, 4096], P(None, 'row', 'col'), may hold values from -0.5 to 8, as said below
Outputs:
- factored: float32 [4, 8192, 4096], P(None, 'row', 'col')
Inputs may be any that keep to these rules, and one draw needn't show every extreme that they name: `choi`: the leading 4096 x 4096 block of the matrix is symmetric with a positive diagonal, and its leading 2 * 256 square is positive definite.
All inputs are finite; a program needn't handle non-finite values.
Results may differ from a plain program's by a relative error of at most 0.0001.
Values sent between devices are 32-bit elements; how exact they have to be, the bound alone decides.
No kernel may reach another device: no remote copies, remote signals or barrier semaphores. Data moves between devices by JAX's collectives and lax.ppermute only.
A program may use at most 64 MiB of HBM per device.

v0:
```python
import jax
import jax.numpy as jnp
from jax import lax
from jax.sharding import Mesh
from jax.sharding import PartitionSpec as P

PANELS = 2
ROW = ("row_0", "row_1")
COL = ("col_0", "col_1")
ROW_COL = ("row_0", "row_1", "col_0", "col_1")


def picked(array, axis, root):
    return lax.dynamic_index_in_dim(lax.all_gather(array, axis), root, 0, keepdims=False)


def from_root(array, axes, root):
    array = jnp.where(lax.axis_index(axes) == root, array, jnp.zeros_like(array))
    for axis in axes:
        array = lax.psum(array, axis)
    return array


def factor_tile(diagonal):
    tile_size = diagonal.shape[0]
    identity = jnp.eye(tile_size, dtype=jnp.float32)
    factor = jnp.linalg.cholesky(diagonal)
    inverse = jax.scipy.linalg.solve_triangular(factor, identity, lower=True)
    return (factor, inverse)


def panel_from(blocks, factor, inverse, tile_index, step):
    beneath = jnp.einsum("sij,kj->sik", blocks, inverse, precision=lax.Precision.HIGHEST)
    place = tile_index[:, None, None]
    return jnp.where(place > step, beneath, jnp.where(place == step, factor[None], 0.0))


def body(choi):
    slot_count = choi.shape[0]
    row_count = lax.axis_size(ROW)
    col_count = lax.axis_size(COL)
    my_row = lax.axis_index(ROW)
    my_col = lax.axis_index(COL)
    tile_index = jnp.arange(slot_count, dtype=jnp.int32) * row_count + my_row
    current = choi
    for step in range(PANELS):
        row_tile = current[step // row_count]
        tile_row = picked(row_tile, ROW, step % row_count)
        diagonal = from_root(row_tile, ROW_COL, step % row_count * col_count + step)
        raw_tiles = from_root(current, COL, step)
        factor, inverse = factor_tile(diagonal)
        panel_tiles = panel_from(raw_tiles, factor, inverse, tile_index, step)
        partner = jnp.dot(tile_row.T, inverse.T, precision=lax.Precision.HIGHEST)
        updated = current - jnp.einsum(
            "sij,kj->sik", panel_tiles, partner, precision=lax.Precision.HIGHEST
        )
        trailing = (tile_index[:, None, None] > step) & (my_col > step)
        current = jnp.where(my_col == step, panel_tiles, jnp.where(trailing, updated, current))
    cleared = (my_col >= PANELS) & (tile_index[:, None, None] < PANELS)
    return jnp.where(cleared, 0.0, current)


def solution(mesh):
    finer = Mesh(mesh.devices.reshape(8, 4, 8, 2), ("row_0", "row_1", "col_0", "col_1"))
    placed = (P(None, ROW, COL),)
    return jax.shard_map(
        body, mesh=finer, in_specs=placed, out_specs=P(None, ROW, COL), check_vma=False
    )
```

profile of v0, /device:TPU:1, one launch (start us, length us, event | category | flops | bytes accessed | tf_op | source)
XLA Modules:
  0.0 675.9 jit_solution(7422537290769370134)
XLA Ops:
  7.4 1.6 copy.19
  9.8 79.2 %all-reduce.14.cloned.1.call-done = f32[256,256]{0,1:T(8,128)} async-done(((f32[256,256]{0,1:T(8,128)}), f32[256,256]{0,1:T(8,128)}) %all-reduce.14.cloned.1.call-update) | async-done | bytes 262160 | tf_op jit(solution)/shard_map/psum | solution.py:20
  90.1 55.0 %all-reduce.16.cloned.1.call-done = f32[256,256]{0,1:T(8,128)} async-done(((f32[256,256]{0,1:T(8,128)}), f32[256,256]{0,1:T(8,128)}) %all-reduce.16.cloned.1.call-update) | async-done | bytes 262160 | tf_op jit(solution)/shard_map/psum | solution.py:20
  145.2 84.3 %all-reduce.24.cloned.1.call-done = (f32[4,256,256]{1,2,0:T(8,128)}, f32[256,256]{0,1:T(8,128)}) async-done(((f32[4,256,256]{1,2,0:T(8,128)}, f32[256,256]{0,1:T(8,128)}), (f32[4,256,256]{1,2,0:T(8,128)}, f32[256,256]{0,1:T(8,128)})) %all-reduce.24.cloned.1.call-update) | async-done | bytes 1310736 | tf_op jit(solution)/shard_map/psum | solution.py:20
  230.6 42.0 %all-reduce.28.cloned.1.call-done = (f32[4,256,256]{1,2,0:T(8,128)}, f32[256,256]{0,1:T(8,128)}) async-done(((f32[4,256,256]{1,2,0:T(8,128)}, f32[256,256]{0,1:T(8,128)}), (f32[4,256,256]{1,2,0:T(8,128)}, f32[256,256]{0,1:T(8,128)})) %all-reduce.28.cloned.1.call-update) | async-done | bytes 1310736 | tf_op jit(solution)/shard_map/psum | solution.py:20
  274.7 11.7 %cholesky.130 = f32[128,128]{1,0:T(8,128)S(1)} custom-call(f32[128,128]{1,0:T(8,128)S(1)} %cholesky.194), custom_call_target="Cholesky" | custom-call | tf_op jit(solution)/shard_map/jit(cholesky)/cholesky | solution.py:27
  286.5 9.8 %custom-call.13 = f32[1,128,128]{1,2,0:T(8,128)S(1)} custom-call(f32[1,128,128]{2,1,0:T(8,128)S(1)} %get-tuple-element.66), custom_call_target="InvertDiagBlocksLowerTriangular" | custom-call | tf_op jit(solution)/shard_map/jit(cholesky)/cholesky | solution.py:27
  296.8 11.7 %cholesky.147 = f32[128,128]{1,0:T(8,128)S(1)} custom-call(f32[128,128]{1,0:T(8,128)S(1)} %convolution_subtract_fusion.3), custom_call_target="Cholesky" | custom-call | tf_op jit(solution)/shard_map/jit(cholesky)/cholesky | solution.py:27
  310.6 4.0 while.4
  314.6 19.7 %custom-call.14 = f32[2,128,128]{1,2,0:T(8,128)S(1)} custom-call(f32[2,128,128]{2,1,0:T(8,128)S(1)} %get-tuple-element.21), custom_call_target="InvertDiagBlocksLowerTriangular" | custom-call | tf_op jit(solution)/shard_map/jit(_solve_triangular)/triangular_solve | solution.py:28
  335.2 2.3 convolution_select_fusion.1
  337.5 1.6 all-gather.3.cloned.1.call-done
  340.5 2.3 broadcast_select_fusion
  343.6 71.4 %all-reduce.18.cloned.1.call-done = f32[256,256]{0,1:T(8,128)} async-done(((f32[256,256]{0,1:T(8,128)}), f32[256,256]{0,1:T(8,128)}) %all-reduce.18.cloned.1.call-update) | async-done | bytes 262160 | tf_op jit(solution)/shard_map/psum | solution.py:20
  415.0 55.8 %all-reduce.20.cloned.1.call-done = f32[256,256]{0,1:T(8,128)} async-done(((f32[256,256]{0,1:T(8,128)}), f32[256,256]{0,1:T(8,128)}) %all-reduce.20.cloned.1.call-update) | async-done | bytes 262160 | tf_op jit(solution)/shard_map/psum | solution.py:20
  470.9 84.4 %all-reduce.22.cloned.1.call-done = (f32[4,256,256]{1,2,0:T(8,128)}, f32[256,256]{0,1:T(8,128)}) async-done(((f32[4,256,256]{1,2,0:T(8,128)}, f32[256,256]{0,1:T(8,128)}), (f32[4,256,256]{1,2,0:T(8,128)}, f32[256,256]{0,1:T(8,128)})) %all-reduce.22.cloned.1.call-update) | async-done | bytes 1310736 | tf_op jit(solution)/shard_map/psum | solution.py:20
  556.2 42.5 %all-reduce.26.cloned.1.call-done = (f32[4,256,256]{1,2,0:T(8,128)}, f32[256,256]{0,1:T(8,128)}) async-done(((f32[4,256,256]{1,2,0:T(8,128)}, f32[256,256]{0,1:T(8,128)}), (f32[4,256,256]{1,2,0:T(8,128)}, f32[256,256]{0,1:T(8,128)})) %all-reduce.26.cloned.1.call-update) | async-done | bytes 1310736 | tf_op jit(solution)/shard_map/psum | solution.py:20
  600.8 11.7 %cholesky.164 = f32[128,128]{1,0:T(8,128)S(1)} custom-call(f32[128,128]{1,0:T(8,128)S(1)} %cholesky.197), custom_call_target="Cholesky" | custom-call | tf_op jit(solution)/shard_map/jit(cholesky)/cholesky | solution.py:27
  612.6 9.8 %custom-call.15 = f32[1,128,128]{1,2,0:T(8,128)S(1)} custom-call(f32[1,128,128]{2,1,0:T(8,128)S(1)} %get-tuple-element.62), custom_call_target="InvertDiagBlocksLowerTriangular" | custom-call | tf_op jit(solution)/shard_map/jit(cholesky)/cholesky | solution.py:27
  622.9 11.7 %cholesky.181 = f32[128,128]{1,0:T(8,128)S(1)} custom-call(f32[128,128]{1,0:T(8,128)S(1)} %convolution_subtract_fusion.2), custom_call_target="Cholesky" | custom-call | tf_op jit(solution)/shard_map/jit(cholesky)/cholesky | solution.py:27
  637.3 4.0 while.5
  641.3 19.7 %custom-call.16 = f32[2,128,128]{1,2,0:T(8,128)S(1)} custom-call(f32[2,128,128]{2,1,0:T(8,128)S(1)} %get-tuple-element.22), custom_call_target="InvertDiagBlocksLowerTriangular" | custom-call | tf_op jit(solution)/shard_map/jit(_solve_triangular)/triangular_solve | solution.py:28
  661.9 2.3 convolution_select_fusion
  664.4 1.5 convolution_bitcast_fusion
  (79 shorter events, 25.7 us)
Async XLA Ops:
  7.4 81.6 %all-reduce.14.cloned.1.call-start = ((), (), s32[]{:S(2)}) async-start(), calls=%async_computation | async-start | bytes 524288 | tf_op jit(solution)/shard_map/psum | solution.py:20
  9.7 135.4 %all-reduce.16.cloned.1.call-start = ((), (), s32[]{:S(2)}) async-start(), calls=%async_computation.1 | async-start | bytes 524288 | tf_op jit(solution)/shard_map/psum | solution.py:20
  89.0 140.5 %all-reduce.24.cloned.1.call-start = ((), (), s32[]{:S(2)}) async-start(), calls=%async_computation.7 | async-start | bytes 2621440 | tf_op jit(solution)/shard_map/psum | solution.py:20
  145.2 127.5 %all-reduce.28.cloned.1.call-start = ((), (), s32[]{:S(2)}) async-start(), calls=%async_computation.9 | async-start | bytes 2621440 | tf_op jit(solution)/shard_map/psum | solution.py:20
  229.5 109.6 %all-gather.3.cloned.1.call-start = ((), (), s32[]{:S(2)}) async-start(), calls=%async_computation.2 | async-start | bytes 8650752 | tf_op jit(solution)/shard_map/all_gather | solution.py:14
  230.5 184.5 %all-reduce.18.cloned.1.call-start = ((), (), s32[]{:S(2)}) async-start(), calls=%async_computation.3 | async-start | bytes 524288 | tf_op jit(solution)/shard_map/psum | solution.py:20
  343.5 127.3 %all-reduce.20.cloned.1.call-start = ((), (), s32[]{:S(2)}) async-start(), calls=%async_computation.4 | async-start | bytes 524288 | tf_op jit(solution)/shard_map/psum | solution.py:20
  414.9 140.3 %all-reduce.22.cloned.1.call-start = ((), (), s32[]{:S(2)}) async-start(), calls=%async_computation.6 | async-start | bytes 2621440 | tf_op jit(solution)/shard_map/psum | solution.py:20
  470.8 127.9 %all-reduce.26.cloned.1.call-start = ((), (), s32[]{:S(2)}) async-start(), calls=%async_computation.8 | async-start | bytes 2621440 | tf_op jit(solution)/shard_map/psum | solution.py:20
  555.3 109.1 %all-gather.5.cloned.1.call-start = ((), (), s32[]{:S(2)}) async-start(), calls=%async_computation.5 | async-start | bytes 8650752 | tf_op jit(solution)/shard_map/all_gather | solution.py:14
Sparse Core Ops, SparseCore 0:
  10.5 78.4 all-reduce.13
  91.4 53.6 all-reduce.15
  147.6 81.9 all-reduce.23
  232.3 40.2 all-reduce.27
  343.6 71.2 all-reduce.17
  417.1 53.6 all-reduce.19
  473.4 81.8 all-reduce.21
  558.4 40.2 all-reduce.25
Sparse Core Ops, SparseCore 1:
  233.7 105.4 all-gather.2
  558.9 105.4 all-gather.4
where the time goes:
time: 676 us
  waiting for transfers between devices  517 us (76%)
  other arithmetic  113 us (17%)
  between operations  17.7 us (3%)
  local copies, waits for them, and re-layouts  14.6 us (2%)
  matrix products  13.7 us (2%)
    psum x8, waiting for transfers between devices, from_root(): array = lax.psum(array, axis)  515 us
    another operation x13, other arithmetic, factor_tile(): factor = jnp.linalg.cholesky(diagonal)  68.5 us
    another operation x5, other arithmetic, factor_tile(): inverse = jax.scipy.linalg.solve_triangular(factor, identity, lower=True)  39.4 us
  transfers between devices with their start and end apart: 10, of which 10 were waited for; matrix products, arithmetic and copies ran while one was open for 19% of the time, Pallas kernels for 0%

commit v1 on v0

--- a/solution.py
+++ b/solution.py
@@ -17,7 +17,7 @@
 def from_root(array, axes, root):
     array = jnp.where(lax.axis_index(axes) == root, array, jnp.zeros_like(array))
     for axis in axes:
-        array = lax.psum(array, axis)
+        array = jnp.sum(lax.all_gather(array, axis), axis=0)
     return array
 
 

time: 676 us -> 728 us (1.077)
  other arithmetic: 113 us -> 138 us
  waiting for transfers between devices: 517 us -> 532 us
  blocking collectives: 0 us -> 13.6 us
    psum x8 -> x0, waiting for transfers between devices: 515 us -> none  [from_root(): array = lax.psum(array, axis)]
    all_gather x0 -> x10, waiting for transfers between devices: none -> 409 us  [from_root(): array = jnp.sum(lax.all_gather(array, axis), axis=0)]
    all_gather x2, waiting for transfers between devices: 1.72 us -> 121 us  [picked(): lax.all_gather(array, axis)]
    reduce_sum x0 -> x12, other arithmetic: none -> 26.4 us  [from_root(): array = jnp.sum(lax.all_gather(array, axis), axis=0)]
    all_gather x0 -> x2, blocking collectives: none -> 13.6 us  [from_root(): array = jnp.sum(lax.all_gather(array, axis), axis=0)]
  transfers between devices with their start and end apart: 10 -> 12, of which waited for: 10 -> 12; matrix products, arithmetic and copies ran while one was open for 19% -> 19% of each run, Pallas kernels for 0% -> 0%
where the time goes in v1:
time: 728 us; the launch traced here: 721 us
  waiting for transfers between devices  532 us (73%)
  other arithmetic  138 us (19%)
  between operations  16.5 us (2%)
  blocking collectives  13.6 us (2%)
  matrix products  11.6 us (2%)
  local copies, waits for them, and re-layouts  7.96 us (1%)
    all_gather x10, waiting for transfers between devices, from_root(): array = jnp.sum(lax.all_gather(array, axis), axis=0)  409 us
    all_gather x2, waiting for transfers between devices, picked(): lax.all_gather(array, axis)  121 us
    another operation x13, other arithmetic, factor_tile(): factor = jnp.linalg.cholesky(diagonal)  68.5 us
    another operation x5, other arithmetic, factor_tile(): inverse = jax.scipy.linalg.solve_triangular(factor, identity, lower=True)  39.4 us
    reduce_sum x12, other arithmetic, from_root(): array = jnp.sum(lax.all_gather(array, axis), axis=0)  26.4 us
  transfers between devices with their start and end apart: 12, of which 12 were waited for; matrix products, arithmetic and copies ran while one was open for 19% of the time, Pallas kernels for 0%

profile of v1, /device:TPU:1, one launch (start us, length us, event | category | flops | bytes accessed | tf_op | source)
XLA Modules:
  0.0 721.1 jit_solution(4719541552113364527)
XLA Ops:
  8.4 46.5 %all-gather.23.cloned.1.call-done = f32[8,256,256]{2,1,0:T(8,128)} async-done(((f32[1,256,256]{2,1,0:T(8,128)}), f32[8,256,256]{2,1,0:T(8,128)}) %all-gather.23.cloned.1.call-update) | async-done | bytes 2097168 | tf_op jit(solution)/shard_map/all_gather | solution.py:20
  57.4 31.3 %all-gather.35.cloned.1.call-done = f32[1024,256]{1,0:T(8,128)} async-done(((f32[256,256]{1,0:T(8,128)}), f32[1024,256]{1,0:T(8,128)}) %all-gather.35.cloned.1.call-update) | async-done | bytes 1048592 | tf_op jit(solution)/shard_map/all_gather | solution.py:20
  92.6 40.1 %all-gather.37.cloned.1.call-done = f32[2048,256]{1,0:T(8,128)} async-done(((f32[256,256]{1,0:T(8,128)}), f32[2048,256]{1,0:T(8,128)}) %all-gather.37.cloned.1.call-update) | async-done | bytes 2097168 | tf_op jit(solution)/shard_map/all_gather | solution.py:20
  134.5 6.5 all-gather.4
  141.3 11.7 %cholesky.130 = f32[128,128]{1,0:T(8,128)S(1)} custom-call(f32[128,128]{1,0:T(8,128)S(1)} %cholesky.194), custom_call_target="Cholesky" | custom-call | tf_op jit(solution)/shard_map/jit(cholesky)/cholesky | solution.py:27
  153.1 9.8 %custom-call.13 = f32[1,128,128]{1,2,0:T(8,128)S(1)} custom-call(f32[1,128,128]{2,1,0:T(8,128)S(1)} %get-tuple-element.58), custom_call_target="InvertDiagBlocksLowerTriangular" | custom-call | tf_op jit(solution)/shard_map/jit(cholesky)/cholesky | solution.py:27
  163.1 71.4 %all-gather.31.cloned.1.call-done = f32[32,256,256]{2,1,0:T(8,128)} async-done(((f32[4,256,256]{2,1,0:T(8,128)}), f32[32,256,256]{2,1,0:T(8,128)}) %all-gather.31.cloned.1.call-update) | async-done | bytes 8388624 | tf_op jit(solution)/shard_map/all_gather | solution.py:20
  234.5 5.1 reduce_sum.108
  240.2 11.7 %cholesky.147 = f32[128,128]{1,0:T(8,128)S(1)} custom-call(f32[128,128]{1,0:T(8,128)S(1)} %convolution_subtract_fusion.3), custom_call_target="Cholesky" | custom-call | tf_op jit(solution)/shard_map/jit(cholesky)/cholesky | solution.py:27
  257.8 19.7 %custom-call.14 = f32[2,128,128]{1,2,0:T(8,128)S(1)} custom-call(f32[2,128,128]{2,1,0:T(8,128)S(1)} %get-tuple-element.21), custom_call_target="InvertDiagBlocksLowerTriangular" | custom-call | tf_op jit(solution)/shard_map/jit(_solve_triangular)/triangular_solve | solution.py:28
  278.4 60.7 %all-gather.25.cloned.1.call-done = f32[32,256,256]{2,1,0:T(8,128)} async-done(((f32[1,256,256]{2,1,0:T(8,128)}), f32[32,256,256]{2,1,0:T(8,128)}) %all-gather.25.cloned.1.call-update) | async-done | bytes 8388624 | tf_op jit(solution)/shard_map/all_gather | solution.py:14
  340.4 18.8 %all-gather.33.cloned.1.call-done = f32[8,256,256]{2,1,0:T(8,128)} async-done(((f32[4,256,256]{2,1,0:T(8,128)}), f32[8,256,256]{2,1,0:T(8,128)}) %all-gather.33.cloned.1.call-update) | async-done | bytes 2097168 | tf_op jit(solution)/shard_map/all_gather | solution.py:20
  365.1 39.9 %all-gather.27.cloned.1.call-done = f32[8,256,256]{2,1,0:T(8,128)} async-done(((f32[1,256,256]{2,1,0:T(8,128)}), f32[8,256,256]{2,1,0:T(8,128)}) %all-gather.27.cloned.1.call-update) | async-done | bytes 2097168 | tf_op jit(solution)/shard_map/all_gather | solution.py:20
  407.5 31.3 %all-gather.43.cloned.1.call-done = f32[1024,256]{1,0:T(8,128)} async-done(((f32[256,256]{1,0:T(8,128)}), f32[1024,256]{1,0:T(8,128)}) %all-gather.43.cloned.1.call-update) | async-done | bytes 1048592 | tf_op jit(solution)/shard_map/all_gather | solution.py:20
  442.2 40.6 %all-gather.45.cloned.1.call-done = f32[2048,256]{1,0:T(8,128)} async-done(((f32[256,256]{1,0:T(8,128)}), f32[2048,256]{1,0:T(8,128)}) %all-gather.45.cloned.1.call-update) | async-done | bytes 2097168 | tf_op jit(solution)/shard_map/all_gather | solution.py:20
  484.6 7.0 all-gather.9
  491.9 11.7 %cholesky.164 = f32[128,128]{1,0:T(8,128)S(1)} custom-call(f32[128,128]{1,0:T(8,128)S(1)} %cholesky.197), custom_call_target="Cholesky" | custom-call | tf_op jit(solution)/shard_map/jit(cholesky)/cholesky | solution.py:27
  503.6 9.8 %custom-call.15 = f32[1,128,128]{1,2,0:T(8,128)S(1)} custom-call(f32[1,128,128]{2,1,0:T(8,128)S(1)} %get-tuple-element.54), custom_call_target="InvertDiagBlocksLowerTriangular" | custom-call | tf_op jit(solution)/shard_map/jit(cholesky)/cholesky | solution.py:27
  513.9 70.8 %all-gather.39.cloned.1.call-done = f32[32,256,256]{2,1,0:T(8,128)} async-done(((f32[4,256,256]{2,1,0:T(8,128)}), f32[32,256,256]{2,1,0:T(8,128)}) %all-gather.39.cloned.1.call-update) | async-done | bytes 8388624 | tf_op jit(solution)/shard_map/all_gather | solution.py:20
  584.7 5.0 reduce_sum.114
  590.4 11.7 %cholesky.181 = f32[128,128]{1,0:T(8,128)S(1)} custom-call(f32[128,128]{1,0:T(8,128)S(1)} %convolution_subtract_fusion.2), custom_call_target="Cholesky" | custom-call | tf_op jit(solution)/shard_map/jit(cholesky)/cholesky | solution.py:27
  608.0 19.7 %custom-call.16 = f32[2,128,128]{1,2,0:T(8,128)S(1)} custom-call(f32[2,128,128]{2,1,0:T(8,128)S(1)} %get-tuple-element.22), custom_call_target="InvertDiagBlocksLowerTriangular" | custom-call | tf_op jit(solution)/shard_map/jit(_solve_triangular)/triangular_solve | solution.py:28
  628.6 60.4 %all-gather.29.cloned.1.call-done = f32[32,256,256]{2,1,0:T(8,128)} async-done(((f32[1,256,256]{2,1,0:T(8,128)}), f32[32,256,256]{2,1,0:T(8,128)}) %all-gather.29.cloned.1.call-update) | async-done | bytes 8388624 | tf_op jit(solution)/shard_map/all_gather | solution.py:14
  690.6 18.6 %all-gather.41.cloned.1.call-done = f32[8,256,256]{2,1,0:T(8,128)} async-done(((f32[4,256,256]{2,1,0:T(8,128)}), f32[8,256,256]{2,1,0:T(8,128)}) %all-gather.41.cloned.1.call-update) | async-done | bytes 2097168 | tf_op jit(solution)/shard_map/all_gather | solution.py:20
  (95 shorter events, 52.3 us)
Async XLA Ops:
  6.5 48.3 %all-gather.23.cloned.1.call-start = ((), (), s32[]{:S(2)}) async-start(), calls=%async_computation | async-start | bytes 2359296 | tf_op jit(solution)/shard_map/all_gather | solution.py:20
  8.3 80.4 %all-gather.35.cloned.1.call-start = ((), (), s32[]{:S(2)}) async-start(), calls=%async_computation.6 | async-start | bytes 1310720 | tf_op jit(solution)/shard_map/all_gather | solution.py:20
  57.3 75.4 %all-gather.37.cloned.1.call-start = ((), (), s32[]{:S(2)}) async-start(), calls=%async_computation.7 | async-start | bytes 2359296 | tf_op jit(solution)/shard_map/all_gather | solution.py:20
  90.8 143.8 %all-gather.31.cloned.1.call-start = ((), (), s32[]{:S(2)}) async-start(), calls=%async_computation.4 | async-start | bytes 9437184 | tf_op jit(solution)/shard_map/all_gather | solution.py:20
  91.9 247.2 %all-gather.25.cloned.1.call-start = ((), (), s32[]{:S(2)}) async-start(), calls=%async_computation.1 | async-start | bytes 8650752 | tf_op jit(solution)/shard_map/all_gather | solution.py:14
  92.5 266.7 %all-gather.33.cloned.1.call-start = ((), (), s32[]{:S(2)}) async-start(), calls=%async_computation.5 | async-start | bytes 3145728 | tf_op jit(solution)/shard_map/all_gather | solution.py:20
  234.5 127.6 %copy-start = (f32[4,256,256]{2,1,0:T(8,128)S(1)}, f32[4,256,256]{2,1,0:T(8,128)}, u32[]{:S(2)}) copy-start(f32[4,256,256]{2,1,0:T(8,128)} %param.4) | copy-start | bytes 3145732
  239.7 165.2 %all-gather.27.cloned.1.call-start = ((), (), s32[]{:S(2)}) async-start(), calls=%async_computation.2 | async-start | bytes 2359296 | tf_op jit(solution)/shard_map/all_gather | solution.py:20
  365.0 73.8 %all-gather.43.cloned.1.call-start = ((), (), s32[]{:S(2)}) async-start(), calls=%async_computation.10 | async-start | bytes 1310720 | tf_op jit(solution)/shard_map/all_gather | solution.py:20
  407.4 75.4 %all-gather.45.cloned.1.call-start = ((), (), s32[]{:S(2)}) async-start(), calls=%async_computation.11 | async-start | bytes 2359296 | tf_op jit(solution)/shard_map/all_gather | solution.py:20
  440.8 143.9 %all-gather.39.cloned.1.call-start = ((), (), s32[]{:S(2)}) async-start(), calls=%async_computation.8 | async-start | bytes 9437184 | tf_op jit(solution)/shard_map/all_gather | solution.py:20
  441.4 247.6 %all-gather.29.cloned.1.call-start = ((), (), s32[]{:S(2)}) async-start(), calls=%async_computation.3 | async-start | bytes 8650752 | tf_op jit(solution)/shard_map/all_gather | solution.py:14
  442.2 267.0 %all-gather.41.cloned.1.call-start = ((), (), s32[]{:S(2)}) async-start(), calls=%async_computation.9 | async-start | bytes 3145728 | tf_op jit(solution)/shard_map/all_gather | solution.py:20
Sparse Core Ops, SparseCore 0:
  9.4 45.3 all-gather.22
  57.5 31.1 all-gather.34
  90.9 41.8 all-gather.36
  134.7 99.7 all-gather.30
  237.5 101.4 all-gather.24
  341.0 18.1 all-gather.32
  365.1 39.7 all-gather.26
  407.5 31.1 all-gather.42
  440.9 41.8 all-gather.44
  484.8 99.8 all-gather.38
  587.9 101.1 all-gather.28
  691.0 18.1 all-gather.40
